TPU v7x, 32 devices: a whole 2x2x4 slice. The times are simulated.
32 devices in a mesh: vol: 2 (over y), space: 16 (over z, x, core).
Axes of the slice: x: 2, y: 2, z: 4, core: 2. Of those that a mesh axis runs over, the one named last changes fastest.
Arguments:
- volume: bfloat16 [2, 32, 64, 8, 128], P('vol', None, 'space'), may hold values from -80 to 80
- conv_weight: bfloat16 [32, 32, 3, 3, 3], replicated, may hold values from -0.21875 to 0.21875
- conv_bias: float32 [32], replicated, may hold values from -3 to 3
- basis: float32 [864, 864], replicated, may hold values from -3 to 3
- damping: float32 [1], replicated, may hold values from 0.5 to 2
Outputs:
- projected: float32 [864, 864], P('vol')
All inputs are finite; a program needn't handle non-finite values.
Results may differ from a plain program's by a relative error of at most 0.0019.
Values may be sent and summed in bfloat16 or wider, within the bound.
A program may use at most 64 MiB of HBM per device.

v0:
```python
import jax
import jax.numpy as jnp
from jax import lax
from jax.sharding import PartitionSpec as P


def shifted(block, axis, distance):
    devices = range(lax.axis_size(axis))
    route = [(i - distance, i) for i in devices if i - distance in devices]
    return lax.ppermute(block, axis, route)


def extract_patches(activated):
    chans, planes, rows_y, cols_z = activated.shape
    viewed = activated.reshape(chans, planes // 4, 4, rows_y // 4, 4, cols_z // 4, 4)[
        :, :, 1:, :, 1:, :, 1:
    ]
    viewed = viewed.transpose(0, 2, 4, 6, 1, 3, 5)
    return viewed.reshape(chans * 27, -1)


def body(volume, conv_weight, conv_bias, basis, damping):
    local_block = volume[0]
    from_above = shifted(local_block[:, 0:1], "space", -1)
    zero_plane = jnp.zeros_like(from_above)
    stacked = jnp.concatenate([zero_plane, local_block, from_above], axis=1)
    conv_out = lax.conv_general_dilated(
        stacked[None],
        conv_weight,
        (1, 1, 1),
        [(0, 0), (1, 1), (1, 1)],
        dimension_numbers=("NCDHW", "OIDHW", "NCDHW"),
        preferred_element_type=jnp.float32,
    )[0]
    activated = jnp.maximum(conv_out + conv_bias[:, None, None, None], 0.0).astype(jnp.bfloat16)
    patch_cols = extract_patches(activated)
    local_gram = jnp.dot(patch_cols, patch_cols.T, preferred_element_type=jnp.float32)
    gram_width = local_gram.shape[0]
    total_patches = patch_cols.shape[1] * lax.axis_size("space") * lax.axis_size("vol")
    panel_rows = gram_width // lax.axis_size("vol")
    row_start = lax.axis_index("vol") * panel_rows
    partial_rows = lax.psum_scatter(
        local_gram.astype(jnp.bfloat16), "vol", scatter_dimension=0, tiled=True
    ).astype(jnp.float32)
    row_panel = lax.psum(partial_rows, "space")
    diag_block = lax.dynamic_slice_in_dim(row_panel, row_start, panel_rows, 1)
    trace_value = lax.psum(jnp.trace(diag_block), "vol")
    normed_panel = row_panel / total_patches
    mean_diagonal = trace_value / total_patches / gram_width
    basis_rows = lax.dynamic_slice_in_dim(basis, row_start, panel_rows, 0)
    product = jnp.dot(
        normed_panel, basis, precision=lax.Precision.HIGHEST, preferred_element_type=jnp.float32
    )
    return product + damping[0] * mean_diagonal * basis_rows


def solution(mesh):
    in_specs = (P("vol", None, "space", None, None), P(), P(), P(), P())
    out_specs = P("vol", None)
    return jax.shard_map(body, mesh=mesh, in_specs=in_specs, out_specs=out_specs, check_vma=False)
```

profile of v0, /device:TPU:0, one launch (start us, length us, event | category | flops | bytes accessed | tf_op | source)
XLA Modules:
  0.0 149.4 jit_solution(2289497347999911215)
XLA Ops:
  6.5 0.0 copy-start
  6.5 0.0 reduce-scatter.2.cloned.1.call-start
  6.5 0.9 slice.10
  7.4 1.3 collective-permute-start
  8.7 1.8 %collective-permute-done = bf16[32,1,8,128]{3,2,1,0:T(8,128)(2,1)S(1)} collective-permute-done((bf16[32,1,8,128]{3,2,1,0:T(8,128)(2,1)S(1)}, bf16[32,1,8,128]{3,2,1,0:T(8,128)(2,1)S(1)}, u32[]{:S(2)}, u32[]{:S(2)}) %collective-permute-start) | collective-permute-done | bytes 65568 | tf_op jit(solution)/shard_map/ppermute | solution.py:10
  10.6 1.1 pad_maximum_fusion
  11.6 1.0 copy.21
  12.6 0.3 pad
  12.9 0.0 copy-start.2
  12.9 0.2 copy.23
  13.2 0.1 slice.11
  13.2 0.0 copy-done
  13.2 0.4 copy-done.2
  13.6 3.9 %fusion.10 = f32[4,8,8,17,32]{4,2,3,1,0:T(8,128)S(1)} fusion(bf16[32,32,3,3,3]{1,0,4,3,2:T(8,128)(2,1)S(1)} %copy-done, bf16[32,6,8,1,7,2]{0,4,5,2,1,3:T(8,128)(2,1)S(1)} %slice.11, bf16[32,6,8,1,8,17]{0,4,5,2,1,3:T(8,128)(2,1)S(1)} %copy.23, pred[8,17]{0,1:T(8,128)(4,1)S(1)} %copy-done.2), kind=kOutput, calls=%fused_computation.12 | convolution fusion | flops 222134272 | bytes 1073288 | tf_op jit(solution)/shard_map/conv_general_dilated | solution.py:27
  17.5 0.4 copy.24
  17.9 0.1 slice.12
  18.0 0.0 copy-start.1
  18.0 0.3 slice.13
  18.4 0.6 copy.30
  19.0 0.0 copy-done.1
  19.0 0.2 fusion.17
  19.2 0.3 copy.27
  19.5 0.2 reshape.21
  19.8 1.7 %convolution_convert_fusion = bf16[864,864]{1,0:T(8,128)(2,1)} fusion(bf16[864,64]{1,0:T(8,128)(2,1)S(1)} %reshape.21), kind=kOutput, calls=%fused_computation.8 | convolution fusion | flops 96297984 | bytes 1603584 | tf_op jit(solution)/shard_map/dot_general | solution.py:37
  21.5 0.0 reduce-scatter.2.cloned.1.call-update
  21.5 30.5 %reduce-scatter.2.cloned.1.call-done = bf16[432,864]{1,0:T(8,128)(2,1)} async-done(((bf16[864,864]{1,0:T(8,128)(2,1)}), bf16[432,864]{1,0:T(8,128)(2,1)}) %reduce-scatter.2.cloned.1.call-update) | async-done | bytes 746512 | tf_op jit(solution)/shard_map/reduce_scatter | solution.py:42
  51.9 74.4 %all-reduce.1 = f32[432,864]{1,0:T(8,128)S(1)} all-reduce(bf16[432,864]{1,0:T(8,128)(2,1)} %reduce-scatter.2.cloned.1.call-done), channel_id=1, replica_groups=mesh['vol'=2,'space'=16] {'space'}, use_global_device_ids=true, to_apply=%region_1.0 | all-reduce | flops 373248 | bytes 2239488 | tf_op jit(solution)/shard_map/psum | solution.py:45
  126.3 0.8 select_reduce_fusion
  127.8 5.5 %psum.15 = f32[]{:T(128)} all-reduce(f32[]{:T(128)} %select_reduce_fusion), channel_id=1, replica_groups=mesh['vol'=2,'space'=16] {'vol'}, use_global_device_ids=true, to_apply=%region_3.4 | all-reduce | flops 1 | bytes 8 | tf_op jit(solution)/shard_map/psum | solution.py:47
  134.0 8.6 %multiply_add_fusion = f32[432,864]{1,0:T(8,128)} fusion(f32[864,864]{1,0:T(8,128)} %param.8, s32[]{:T(128)S(6)} %select_n.9, f32[432,864]{1,0:T(8,128)S(1)} %all-reduce.1, f32[]{:T(128)S(6)} %mul.13), kind=kOutput, calls=%fused_computation.9 | convolution fusion | flops 3870955008 | bytes 7630856 | tf_op jit(solution)/shard_map/dot_general | solution.py:51
  (1 shorter events, 0.0 us)
Async XLA Ops:
  6.5 6.7 %copy-start = (bf16[32,32,3,3,3]{1,0,4,3,2:T(8,128)(2,1)S(1)}, bf16[32,32,3,3,3]{1,0,4,3,2:T(8,128)(2,1)}, u32[]{:S(2)}) copy-start(bf16[32,32,3,3,3]{1,0,4,3,2:T(8,128)(2,1)} %param.6) | copy-start | bytes 165892
  6.5 45.4 %reduce-scatter.2.cloned.1.call-start = ((), (), s32[]{:S(2)}) async-start(), calls=%async_computation.1 | async-start | bytes 2322432 | tf_op jit(solution)/shard_map/reduce_scatter | solution.py:42
  7.4 3.1 %collective-permute-start = (bf16[32,1,8,128]{3,2,1,0:T(8,128)(2,1)S(1)}, bf16[32,1,8,128]{3,2,1,0:T(8,128)(2,1)S(1)}, u32[]{:S(2)}, u32[]{:S(2)}) collective-permute-start(bf16[32,1,8,128]{3,2,1,0:T(8,128)(2,1)S(1)} %slice.10), channel_id=1, source_target_pairs={{1,0},{2,1},{3,2},{4,3},{5,4},{6,5},{7,6},{8,7},{9,8},{10,9},{11,1... | collective-permute-start | bytes 196616 | tf_op jit(solution)/shard_map/ppermute | solution.py:10
  12.9 0.7 copy-start.2
  18.0 1.0 copy-start.1
Sparse Core Ops, SparseCore 0:
  21.6 30.2 reduce-scatter.1
where the time goes:
time: 150 us; the launch traced here: 149 us
  blocking collectives  79.9 us (53%)
  waiting for transfers between devices  32.3 us (22%)
  between operations  14.9 us (10%)
  matrix products  14.1 us (9%)
  local copies, waits for them, and re-layouts  4.89 us (3%)
  other arithmetic  2.03 us (1%)
    psum x1, blocking collectives, body(): row_panel = lax.psum(partial_rows, 'space')  74.4 us
    reduce_scatter x1, waiting for transfers between devices, body(): lax.psum_scatter(local_gram.astype(jnp.bfloat16), 'vol', scatter_dimensio...  30.5 us
    dot_general x1, matrix products, body(): jnp.dot(normed_panel, basis, precision=lax.Precision.HIGHEST, preferred_e...  8.56 us
    psum x1, blocking collectives, body(): trace_value = lax.psum(jnp.trace(diag_block), 'vol')  5.53 us
    conv_general_dilated x1, matrix products, body(): lax.conv_general_dilated(stacked[None], conv_weight, (1, 1, 1), [(0, 0),...  3.85 us
  transfers between devices with their start and end apart: 2, of which 2 were waited for; matrix products, arithmetic and copies ran while one was open for 0% of the time, Pallas kernels for 0%

commit v1 on v0

--- a/solution.py
+++ b/solution.py
@@ -42,7 +42,11 @@
     partial_rows = lax.psum_scatter(
         local_gram.astype(jnp.bfloat16), "vol", scatter_dimension=0, tiled=True
     ).astype(jnp.float32)
-    row_panel = lax.psum(partial_rows, "space")
+    row_panel = partial_rows
+    for hop in (1, 2, 4, 8):
+        row_panel = row_panel + lax.ppermute(
+            row_panel, "space", [(dev, dev ^ hop) for dev in range(16)]
+        )
     diag_block = lax.dynamic_slice_in_dim(row_panel, row_start, panel_rows, 1)
     trace_value = lax.psum(jnp.trace(diag_block), "vol")
     normed_panel = row_panel / total_patches

time: 150 us -> 222 us (1.48)
  waiting for transfers between devices: 32.3 us -> 170 us
  blocking collectives: 79.9 us -> 5.48 us
  starting transfers between devices: 1.28 us -> 6.94 us
  other arithmetic: 2.03 us -> 5.53 us
    ppermute x0 -> x4, waiting for transfers between devices: none -> 137 us  [body(): lax.ppermute(row_panel, 'space', [(dev, dev ^ hop) for dev in range(16)])]
    psum x1 -> x0, blocking collectives: 74.4 us -> none  [body(): row_panel = lax.psum(partial_rows, 'space')]
    ppermute x0 -> x4, starting transfers between devices: none -> 5.66 us  [body(): lax.ppermute(row_panel, 'space', [(dev, dev ^ hop) for dev in range(16)])]
    add x0 -> x4, other arithmetic: none -> 2.25 us  [body(): row_panel + lax.ppermute(row_panel, 'space', [(dev, dev ^ hop) for dev in...]
  transfers between devices with their start and end apart: 2 -> 6, of which waited for: 2 -> 6; matrix products, arithmetic and copies ran while one was open for 0% -> 0% of each run, Pallas kernels for 0% -> 0%
where the time goes in v1:
time: 222 us
  waiting for transfers between devices  170 us (77%)
  between operations  14.8 us (7%)
  matrix products  14.3 us (6%)
  starting transfers between devices  6.94 us (3%)
  other arithmetic  5.53 us (2%)
  blocking collectives  5.48 us (2%)
  local copies, waits for them, and re-layouts  4.9 us (2%)
    ppermute x4, waiting for transfers between devices, body(): lax.ppermute(row_panel, 'space', [(dev, dev ^ hop) for dev in range(16)])  137 us
    reduce_scatter x1, waiting for transfers between devices, body(): lax.psum_scatter(local_gram.astype(jnp.bfloat16), 'vol', scatter_dimensio...  30.5 us
    dot_general x1, matrix products, body(): jnp.dot(normed_panel, basis, precision=lax.Precision.HIGHEST, preferred_e...  8.54 us
    ppermute x4, starting transfers between devices, body(): lax.ppermute(row_panel, 'space', [(dev, dev ^ hop) for dev in range(16)])  5.66 us
    psum x1, blocking collectives, body(): trace_value = lax.psum(jnp.trace(diag_block), 'vol')  5.48 us
  transfers between devices with their start and end apart: 6, of which 6 were waited for; matrix products, arithmetic and copies ran while one was open for 0% of the time, Pallas kernels for 0%

profile of v1, /device:TPU:0, one launch (start us, length us, event | category | flops | bytes accessed | tf_op | source)
XLA Modules:
  0.0 221.6 jit_solution(8815232774472478250)
XLA Ops:
  6.5 0.0 copy-start
  6.5 0.0 reduce-scatter.2.cloned.1.call-start
  6.5 0.9 slice.10
  7.4 1.3 collective-permute-start
  8.7 1.8 collective-permute-done
  10.6 1.1 pad_maximum_fusion
  11.6 1.0 copy.21
  12.6 0.3 pad
  12.9 0.0 copy-start.3
  12.9 0.2 copy.23
  13.2 0.1 slice.11
  13.2 0.0 copy-done
  13.2 0.4 copy-done.3
  13.6 4.0 %fusion.10 = f32[4,8,8,17,32]{4,2,3,1,0:T(8,128)S(1)} fusion(bf16[32,32,3,3,3]{1,0,4,3,2:T(8,128)(2,1)S(1)} %copy-done, bf16[32,6,8,1,7,2]{0,4,5,2,1,3:T(8,128)(2,1)S(1)} %slice.11, bf16[32,6,8,1,8,17]{0,4,5,2,1,3:T(8,128)(2,1)S(1)} %copy.23, pred[8,17]{0,1:T(8,128)(4,1)S(1)} %copy-done.3), kind=kOutput, calls=%fused_computation.12 | convolution fusion | flops 222134272 | bytes 1073288 | tf_op jit(solution)/shard_map/conv_general_dilated | solution.py:27
  17.7 0.4 copy.24
  18.1 0.1 slice.12
  18.2 0.3 slice.13
  18.5 0.0 copy-start.2
  18.5 0.6 copy.30
  19.2 0.0 copy-done.2
  19.2 0.2 fusion.17
  19.4 0.3 copy.27
  19.7 0.2 reshape.21
  19.9 1.7 convolution_convert_fusion
  21.6 0.0 reduce-scatter.2.cloned.1.call-update
  21.7 30.5 %reduce-scatter.2.cloned.1.call-done = bf16[432,864]{1,0:T(8,128)(2,1)} async-done(((bf16[864,864]{1,0:T(8,128)(2,1)}), bf16[432,864]{1,0:T(8,128)(2,1)}) %reduce-scatter.2.cloned.1.call-update) | async-done | bytes 746512 | tf_op jit(solution)/shard_map/reduce_scatter | solution.py:42
  52.1 0.0 copy-start.1
  52.1 1.3 convert_element_type.18
  53.4 0.1 collective-permute-start.1
  53.5 3.4 %collective-permute-done.1 = f32[432,864]{1,0:T(8,128)S(1)} collective-permute-done((f32[432,864]{1,0:T(8,128)S(1)}, f32[432,864]{1,0:T(8,128)S(1)}, u32[]{:S(2)}, u32[]{:S(2)}) %collective-permute-start.1) | collective-permute-done | bytes 1493024 | tf_op jit(solution)/shard_map/ppermute | solution.py:47
  56.9 0.0 copy-done.1
  56.9 0.2 convert_add_fusion
  57.0 1.5 collective-permute-start.2
  58.6 34.4 %collective-permute-done.2 = f32[432,864]{1,0:T(8,128)S(1)} collective-permute-done((f32[432,864]{1,0:T(8,128)S(1)}, f32[432,864]{1,0:T(8,128)S(1)}, u32[]{:S(2)}, u32[]{:S(2)}) %collective-permute-start.2) | collective-permute-done | bytes 1493024 | tf_op jit(solution)/shard_map/ppermute | solution.py:47
  93.0 0.2 add.41
  93.2 1.6 collective-permute-start.3
  94.8 33.6 %collective-permute-done.3 = f32[432,864]{1,0:T(8,128)S(1)} collective-permute-done((f32[432,864]{1,0:T(8,128)S(1)}, f32[432,864]{1,0:T(8,128)S(1)}, u32[]{:S(2)}, u32[]{:S(2)}) %collective-permute-start.3) | collective-permute-done | bytes 1493024 | tf_op jit(solution)/shard_map/ppermute | solution.py:47
  128.4 0.2 add.42
  128.6 2.5 %collective-permute-start.4 = (f32[432,864]{1,0:T(8,128)S(1)}, f32[432,864]{1,0:T(8,128)}, u32[]{:S(2)}, u32[]{:S(2)}) collective-permute-start(f32[432,864]{1,0:T(8,128)S(1)} %add.42), channel_id=1, source_target_pairs={{0,8},{1,9},{2,10},{3,11},{4,12},{5,13},{6,14},{7,15},{8,0},{9,1},... | collective-permute-start | bytes 4478984 | tf_op jit(solution)/shard_map/ppermute | solution.py:47
  131.1 65.9 %collective-permute-done.4 = f32[432,864]{1,0:T(8,128)} collective-permute-done((f32[432,864]{1,0:T(8,128)S(1)}, f32[432,864]{1,0:T(8,128)}, u32[]{:S(2)}, u32[]{:S(2)}) %collective-permute-start.4) | collective-permute-done | bytes 1493024 | tf_op jit(solution)/shard_map/ppermute | solution.py:47
  197.0 1.7 add.43
  198.7 0.8 select_reduce_fusion
  200.1 5.5 %psum.7 = f32[]{:T(128)} all-reduce(f32[]{:T(128)} %select_reduce_fusion), channel_id=1, replica_groups=mesh['vol'=2,'space'=16] {'vol'}, use_global_device_ids=true, to_apply=%region_2.3 | all-reduce | flops 1 | bytes 8 | tf_op jit(solution)/shard_map/psum | solution.py:51
  206.2 8.5 %multiply_add_fusion = f32[432,864]{1,0:T(8,128)} fusion(f32[864,864]{1,0:T(8,128)} %param.8, s32[]{:T(128)S(6)} %select_n.9, f32[432,864]{1,0:T(8,128)S(1)} %add.43, f32[]{:T(128)S(6)} %mul.13), kind=kOutput, calls=%fused_computation.9 | convolution fusion | flops 3870955008 | bytes 7630856 | tf_op jit(solution)/shard_map/dot_general | solution.py:55
  (1 shorter events, 0.0 us)
Async XLA Ops:
  6.5 6.7 %copy-start = (bf16[32,32,3,3,3]{1,0,4,3,2:T(8,128)(2,1)S(1)}, bf16[32,32,3,3,3]{1,0,4,3,2:T(8,128)(2,1)}, u32[]{:S(2)}) copy-start(bf16[32,32,3,3,3]{1,0,4,3,2:T(8,128)(2,1)} %param.6) | copy-start | bytes 165892
  6.5 45.6 %reduce-scatter.2.cloned.1.call-start = ((), (), s32[]{:S(2)}) async-start(), calls=%async_computation.1 | async-start | bytes 2322432 | tf_op jit(solution)/shard_map/reduce_scatter | solution.py:42
  7.4 3.1 %collective-permute-start = (bf16[32,1,8,128]{3,2,1,0:T(8,128)(2,1)S(1)}, bf16[32,1,8,128]{3,2,1,0:T(8,128)(2,1)S(1)}, u32[]{:S(2)}, u32[]{:S(2)}) collective-permute-start(bf16[32,1,8,128]{3,2,1,0:T(8,128)(2,1)S(1)} %slice.10), channel_id=1, source_target_pairs={{1,0},{2,1},{3,2},{4,3},{5,4},{6,5},{7,6},{8,7},{9,8},{10,9},{11,1... | collective-permute-start | bytes 196616 | tf_op jit(solution)/shard_map/ppermute | solution.py:10
  12.9 0.7 copy-start.3
  18.5 0.7 copy-start.2
  52.1 4.8 %copy-start.1 = (bf16[432,864]{1,0:T(8,128)(2,1)S(1)}, bf16[432,864]{1,0:T(8,128)(2,1)}, u32[]{:S(2)}) copy-start(bf16[432,864]{1,0:T(8,128)(2,1)} %reduce-scatter.2.cloned.1.call-done) | copy-start | bytes 2239492
  53.4 3.4 %collective-permute-start.1 = (f32[432,864]{1,0:T(8,128)S(1)}, f32[432,864]{1,0:T(8,128)S(1)}, u32[]{:S(2)}, u32[]{:S(2)}) collective-permute-start(f32[432,864]{1,0:T(8,128)S(1)} %convert_element_type.18), channel_id=1, source_target_pairs={{0,1},{1,0},{2,3},{3,2},{4,5},{5,4},{6,7},{7,6},{8,9},{9,8},{10,11... | collective-permute-start | bytes 4478984 | tf_op jit(solution)/shard_map/ppermute | solution.py:47
  57.0 36.0 %collective-permute-start.2 = (f32[432,864]{1,0:T(8,128)S(1)}, f32[432,864]{1,0:T(8,128)S(1)}, u32[]{:S(2)}, u32[]{:S(2)}) collective-permute-start(f32[432,864]{1,0:T(8,128)S(1)} %convert_add_fusion), channel_id=1, source_target_pairs={{0,2},{1,3},{2,0},{3,1},{4,6},{5,7},{6,4},{7,5},{8,10},{9,11},{10,... | collective-permute-start | bytes 4478984 | tf_op jit(solution)/shard_map/ppermute | solution.py:47
  93.2 35.1 %collective-permute-start.3 = (f32[432,864]{1,0:T(8,128)S(1)}, f32[432,864]{1,0:T(8,128)S(1)}, u32[]{:S(2)}, u32[]{:S(2)}) collective-permute-start(f32[432,864]{1,0:T(8,128)S(1)} %add.41), channel_id=1, source_target_pairs={{0,4},{1,5},{2,6},{3,7},{4,0},{5,1},{6,2},{7,3},{8,12},{9,13},{10,... | collective-permute-start | bytes 4478984 | tf_op jit(solution)/shard_map/ppermute | solution.py:47
  128.6 68.4 %collective-permute-start.4 = (f32[432,864]{1,0:T(8,128)S(1)}, f32[432,864]{1,0:T(8,128)}, u32[]{:S(2)}, u32[]{:S(2)}) collective-permute-start(f32[432,864]{1,0:T(8,128)S(1)} %add.42), channel_id=1, source_target_pairs={{0,8},{1,9},{2,10},{3,11},{4,12},{5,13},{6,14},{7,15},{8,0},{9,1},... | collective-permute-start | bytes 4478984 | tf_op jit(solution)/shard_map/ppermute | solution.py:47
Sparse Core Ops, SparseCore 0:
  21.8 30.2 reduce-scatter.1
